TPU v7x, 128 devices: a whole 4x4x4 slice. The times are simulated.
128 devices in a mesh: ctx: 8 (over x, core), tp: 16 (over y, z).
Axes of the slice: x: 4, y: 4, z: 4, core: 2. Of those that a mesh axis runs over, the one named last changes fastest.
Arguments:
- states: bfloat16 [16384, 4096], P('ctx', 'tp'), may hold values from -6 to 6
- picked: int32 [4096], P('ctx'), may hold values from 0 to 2047, as said below
- counts: int32 [8], P('ctx'), may hold values from 64 to 512, as said below
- norm_gain: bfloat16 [4096], P('tp'), may hold values from 0.099609375 to 1.8984375
- router_weight: bfloat16 [4096], P('tp'), may hold values from -0.09375 to 0.09375
- w_query: bfloat16 [4096, 4096], P(None, 'tp'), may hold values from -0.19 to 0.19
- w_key: bfloat16 [4096, 4096], P(None, 'tp'), may hold values from -1.16 to 1.16
- w_value: bfloat16 [4096, 4096], P(None, 'tp'), may hold values from -0.09375 to 0.09375
- w_out: bfloat16 [4096, 4096], P('tp'), may hold values from -1 to 1
- upstream: bfloat16 [16384, 4096], P('ctx', 'tp'), may hold values from -6 to 6
Outputs:
- mixed: bfloat16 [16384, 4096], P('ctx', 'tp')
- grad_states: bfloat16 [16384, 4096], P('ctx', 'tp')
- grad_query: float32 [4096, 4096], P('ctx', 'tp')
- grad_key: float32 [4096, 4096], P('ctx', 'tp')
- grad_value: float32 [4096, 4096], P('ctx', 'tp')
- grad_output_proj: float32 [4096, 4096], P(('tp', 'ctx'))
- grad_gain: float32 [4096], P('tp')
- grad_router: float32 [4096], P('tp')
Inputs may be any that keep to these rules, and one draw needn't show every extreme that they name: `picked`: in the 512 slots of context shard c, the first counts[c] entries are distinct token indices of that shard in strictly ascending order; every later slot holds 2047 and is not live. `counts`: some context shard has exactly 512 picked tokens.
All inputs are finite; a program needn't handle non-finite values.
Results may differ from a plain program's by a relative error of at most 0.02.
Values may be sent and summed in bfloat16 or wider, within the bound.
A program may use at most 128 MiB of HBM per device.

v0:
```python
import jax
import jax.numpy as jnp
from jax import lax
from jax.sharding import PartitionSpec as P

D = 4096
HD = 128


CONTRACT_COLS = (((1,), (1,)), ((), ()))
CONTRACT_ROWS = (((0,), (0,)), ((), ()))


def body(
    states, picked, counts, norm_gain, router_weight, w_query, w_key, w_value, w_out, upstream
):
    capacity = picked.shape[0]
    local_width = w_query.shape[1]
    head_count = local_width // HD
    ctx_pos = lax.axis_index("ctx")
    tp_pos = lax.axis_index("tp")
    scaling = HD ** (-0.5)
    slots = jnp.arange(capacity, dtype=jnp.int32)
    live_slots = slots < counts[0]
    mine_rows = jnp.take(states, picked, axis=0)
    gathered, gain_full, router_full = (
        lax.all_gather(mine_rows, "tp", axis=1, tiled=True),
        lax.all_gather(norm_gain, "tp", axis=0, tiled=True),
        lax.all_gather(router_weight, "tp", axis=0, tiled=True),
    )
    gate_value = jax.nn.sigmoid(jnp.dot(gathered, router_full, preferred_element_type=jnp.float32))
    live_gate = jnp.where(live_slots, gate_value, 0.0)
    gathered_wide = gathered.astype(jnp.float32)
    inverse = lax.rsqrt(jnp.mean(gathered_wide * gathered_wide, axis=1) + 1e-05)
    normed = (gathered_wide * inverse[:, None] * gain_full.astype(jnp.float32)[None, :]).astype(
        jnp.bfloat16
    )
    queries = jnp.dot(normed, w_query, preferred_element_type=jnp.float32).astype(jnp.bfloat16)
    key_local = jnp.dot(normed, w_key, preferred_element_type=jnp.float32).astype(jnp.bfloat16)
    value_local = jnp.dot(normed, w_value, preferred_element_type=jnp.float32).astype(jnp.bfloat16)
    key_rows, value_rows, key_live = (
        lax.all_gather(key_local, "ctx", axis=0, tiled=True),
        lax.all_gather(value_local, "ctx", axis=0, tiled=True),
        lax.all_gather(live_slots.astype(jnp.bfloat16), "ctx", axis=0, tiled=True),
    )
    total_keys = key_rows.shape[0]
    query_heads = queries.reshape(capacity, head_count, HD)
    key_heads = key_rows.reshape(total_keys, head_count, HD)
    value_heads = value_rows.reshape(total_keys, head_count, HD)
    query_pos = ctx_pos * capacity + slots
    key_pos = jnp.arange(total_keys, dtype=jnp.int32)
    allowed = (key_pos[None, :] <= query_pos[:, None]) & (key_live[None, :] > 0)
    scores = (
        jnp.einsum("qhd,khd->hqk", query_heads, key_heads, preferred_element_type=jnp.float32)
        * scaling
    )
    scores = jnp.where(allowed[None], scores, -1e30)
    highest = jnp.max(scores, axis=-1, keepdims=True)
    lifted = jnp.exp(scores - highest)
    attn_probs = (lifted / jnp.sum(lifted, axis=-1, keepdims=True)).astype(jnp.bfloat16)
    attended = (
        jnp.einsum("hqk,khd->qhd", attn_probs, value_heads, preferred_element_type=jnp.float32)
        .astype(jnp.bfloat16)
        .reshape(capacity, local_width)
    )
    partial_out = jnp.dot(attended, w_out, preferred_element_type=jnp.float32)
    block_out = lax.psum_scatter(
        partial_out.astype(jnp.bfloat16), "tp", scatter_dimension=1, tiled=True
    ).astype(jnp.float32)
    mixed = (
        states.astype(jnp.float32)
        .at[picked]
        .add(live_gate[:, None] * block_out)
        .astype(jnp.bfloat16)
    )
    chosen_grad = jnp.take(upstream, picked, axis=0).astype(jnp.float32)
    block_grad = (live_gate[:, None] * chosen_grad).astype(jnp.bfloat16)
    gate_part = jnp.sum(chosen_grad * block_out, axis=1)
    shard_piece = lax.all_gather(block_grad, "tp", axis=1, tiled=True)
    grad_acc = lax.dot_general(
        shard_piece, w_out, CONTRACT_COLS, preferred_element_type=jnp.float32
    )
    weight_term = lax.dot_general(
        attended, shard_piece, CONTRACT_ROWS, preferred_element_type=jnp.float32
    )
    attended_grad = grad_acc.astype(jnp.bfloat16)
    grad_heads = attended_grad.reshape(capacity, head_count, HD)
    prob_grad = jnp.einsum(
        "qhd,khd->hqk", grad_heads, value_heads, preferred_element_type=jnp.float32
    )
    prob_wide = attn_probs.astype(jnp.float32)
    spread = jnp.sum(prob_wide * prob_grad, axis=-1, keepdims=True)
    score_grad = (prob_wide * (prob_grad - spread) * scaling).astype(jnp.bfloat16)
    query_grad = (
        jnp.einsum("hqk,khd->qhd", score_grad, key_heads, preferred_element_type=jnp.float32)
        .astype(jnp.bfloat16)
        .reshape(capacity, local_width)
    )
    key_term = jnp.einsum(
        "hqk,qhd->khd", score_grad, query_heads, preferred_element_type=jnp.float32
    ).reshape(capacity * lax.axis_size("ctx"), local_width)
    value_term = jnp.einsum(
        "hqk,qhd->khd", attn_probs, grad_heads, preferred_element_type=jnp.float32
    ).reshape(capacity * lax.axis_size("ctx"), local_width)
    key_value_grad = lax.psum_scatter(
        jnp.concatenate([key_term, value_term], axis=1).astype(jnp.bfloat16),
        "ctx",
        scatter_dimension=0,
        tiled=True,
    ).astype(jnp.float32)
    key_grad = key_value_grad[:, :local_width].astype(jnp.bfloat16)
    value_grad = key_value_grad[:, local_width:].astype(jnp.bfloat16)
    norm_part = lax.dot_general(
        query_grad, w_query, CONTRACT_COLS, preferred_element_type=jnp.float32
    )
    norm_part = norm_part + lax.dot_general(
        key_grad, w_key, CONTRACT_COLS, preferred_element_type=jnp.float32
    )
    norm_part = norm_part + lax.dot_general(
        value_grad, w_value, CONTRACT_COLS, preferred_element_type=jnp.float32
    )
    mine_wide = mine_rows.astype(jnp.float32)
    gain_mine = norm_gain.astype(jnp.float32)
    normed_full = lax.psum(norm_part.astype(jnp.bfloat16), "tp").astype(jnp.float32)
    gate_dot = lax.psum(gate_part, "tp")
    row_dot = jnp.sum(normed_full * gain_full.astype(jnp.float32)[None, :] * gathered_wide, axis=1)
    normed_grad = lax.dynamic_slice_in_dim(normed_full, tp_pos * local_width, local_width, 1)
    gate_grad = jnp.where(live_slots, gate_dot * gate_value * (1.0 - gate_value), 0.0)
    scaled_grad = normed_grad * gain_mine[None, :]
    rows_grad = (
        inverse[:, None] * scaled_grad
        - mine_wide * (inverse * inverse * inverse * row_dot / D)[:, None]
    )
    rows_grad = rows_grad + gate_grad[:, None] * router_weight.astype(jnp.float32)[None, :]
    rows_grad = jnp.where(live_slots[:, None], rows_grad, 0.0)
    gain_part = jnp.sum(normed_grad * mine_wide * inverse[:, None], axis=0)
    router_part = jnp.sum(gate_grad[:, None] * mine_wide, axis=0)
    grad_gain, grad_router = lax.psum((gain_part, router_part), "ctx")
    grad_states = upstream.astype(jnp.float32).at[picked].add(rows_grad).astype(jnp.bfloat16)
    query_term = lax.dot_general(
        normed, query_grad, CONTRACT_ROWS, preferred_element_type=jnp.float32
    )
    key_term = lax.dot_general(normed, key_grad, CONTRACT_ROWS, preferred_element_type=jnp.float32)
    value_term = lax.dot_general(
        normed, value_grad, CONTRACT_ROWS, preferred_element_type=jnp.float32
    )
    weight_grad = lax.psum_scatter(
        jnp.concatenate([query_term, key_term, value_term], axis=1).astype(jnp.bfloat16),
        "ctx",
        scatter_dimension=0,
        tiled=True,
    ).astype(jnp.float32)
    grad_query = weight_grad[:, :local_width]
    grad_key = weight_grad[:, local_width : 2 * local_width]
    grad_value = weight_grad[:, 2 * local_width :]
    grad_output_proj = lax.psum_scatter(
        weight_term.astype(jnp.bfloat16), "ctx", scatter_dimension=0, tiled=True
    ).astype(jnp.float32)
    return (
        mixed,
        grad_states,
        grad_query,
        grad_key,
        grad_value,
        grad_output_proj,
        grad_gain,
        grad_router,
    )


def solution(mesh):
    placed = (
        P("ctx", "tp"),
        P("ctx"),
        P("ctx"),
        P("tp"),
        P("tp"),
        P(None, "tp"),
        P(None, "tp"),
        P(None, "tp"),
        P("tp", None),
        P("ctx", "tp"),
    )
    return jax.shard_map(
        body,
        mesh=mesh,
        in_specs=placed,
        out_specs=(
            P("ctx", "tp"),
            P("ctx", "tp"),
            P("ctx", "tp"),
            P("ctx", "tp"),
            P("ctx", "tp"),
            P(("tp", "ctx"), None),
            P("tp"),
            P("tp"),
        ),
        check_vma=False,
    )
```

profile of v0, /device:TPU:1, one launch (start us, length us, event | category | flops | bytes accessed | tf_op | source)
XLA Modules:
  0.0 558.1 jit_solution(14492684491898312494)
XLA Ops:
  13.3 20.1 %all-gather.1 = bf16[16,1,256]{2,1,0:T(2,128)(2,1)S(1)} all-gather(bf16[1,1,256]{2,1,0:T(2,128)(2,1)S(1)} %reshape.158), channel_id=1, replica_groups=mesh['ctx'=8,'tp'=16] {'tp'}, dimensions={0}, use_global_device_ids=true | all-gather | bytes 8704 | tf_op jit(solution)/shard_map/all_gather | solution.py:28
  33.4 39.4 %all-gather.8.cloned.1.call-done = bf16[512,4096]{1,0:T(8,128)(2,1)} async-done(((bf16[512,256]{1,0:T(8,128)(2,1)}), bf16[512,4096]{1,0:T(8,128)(2,1)}) %all-gather.8.cloned.1.call-update) | async-done | bytes 4194320 | tf_op jit(solution)/shard_map/all_gather | solution.py:27
  76.3 3.6 convolution_convert_fusion.7
  80.6 13.2 %all-gather.2 = bf16[8,1,512]{2,1,0:T(2,128)(2,1)S(1)} all-gather(bf16[1,1,512]{2,1,0:T(2,128)(2,1)S(1)} %reshape.160), channel_id=1, replica_groups=mesh['ctx'=8,'tp'=16] {'ctx'}, dimensions={0}, use_global_device_ids=true | all-gather | bytes 9216 | tf_op jit(solution)/shard_map/all_gather | solution.py:44
  97.1 5.0 convolution_convert_fusion.9
  102.4 4.5 convolution_convert_fusion.8
  106.9 4.2 copy.47
  111.1 11.3 %fusion.73 = (f32[2,512]{1,0:T(2,128)S(1)}, f32[2,512,4096]{2,1,0:T(8,128)}) fusion(pred[512,4096]{1,0:T(8,128)(4,1)} %fusion.12, bf16[512,2,128]{0,2,1:T(8,128)(2,1)S(1)} %bitcast.87, bf16[4096,2,128]{0,2,1:T(8,128)(2,1)} %bitcast.68), kind=kOutput, calls=%fused_computation.108 | convolution fusion | flops 1090523136 | bytes 21237760 | tf_op jit(solution)/shard_map/sub | solution.py:59
  122.4 9.5 %divide_convert_fusion = bf16[2,512,4096]{2,1,0:T(8,128)(2,1)} fusion(f32[2,512,4096]{2,1,0:T(8,128)} %get-tuple-element.43, f32[2,512]{1,0:T(2,128)S(1)} %get-tuple-element.42), kind=kLoop, calls=%fused_computation.10 | loop fusion | flops 8388608 | bytes 25169920 | tf_op jit(solution)/shard_map/convert_element_type | solution.py:60
  133.4 6.9 %fusion.25 = bf16[2,128,512]{2,1,0:T(8,128)(2,1)S(1)} fusion(bf16[2,512,4096]{2,1,0:T(8,128)(2,1)} %divide_convert_fusion, bf16[4096,256]{1,0:T(8,128)(2,1)} %all-gather.10.cloned.1.call-done), kind=kOutput, calls=%fused_computation.46 | convolution fusion | flops 1073872896 | bytes 10747904 | tf_op jit(solution)/shard_map/hqk,khd->qhd/dot_general | solution.py:62
  147.0 18.8 %all-gather = bf16[16,1,256]{2,1,0:T(2,128)(2,1)S(1)} all-gather(bf16[1,1,256]{2,1,0:T(2,128)(2,1)S(1)} %reshape.156), channel_id=1, replica_groups=mesh['ctx'=8,'tp'=16] {'tp'}, dimensions={0}, use_global_device_ids=true | all-gather | bytes 8704 | tf_op jit(solution)/shard_map/all_gather | solution.py:29
  165.8 3.4 fusion.74
  169.2 51.4 %reduce-scatter.5.cloned.1.call-done = bf16[512,256]{1,0:T(8,128)(2,1)} async-done(((bf16[512,4096]{1,0:T(8,128)(2,1)}), bf16[512,256]{1,0:T(8,128)(2,1)}) %reduce-scatter.5.cloned.1.call-update) | async-done | bytes 262160 | tf_op jit(solution)/shard_map/reduce_scatter | solution.py:67
  223.0 58.1 %all-gather.14.cloned.1.call-done = bf16[512,4096]{1,0:T(8,128)(2,1)} async-done(((bf16[512,256]{1,0:T(8,128)(2,1)}), bf16[512,4096]{1,0:T(8,128)(2,1)}) %all-gather.14.cloned.1.call-update) | async-done | bytes 4194320 | tf_op jit(solution)/shard_map/all_gather | solution.py:79
  281.1 3.5 convolution_convert_fusion.6
  284.6 4.8 convolution_convert_fusion.1
  289.4 8.1 %fusion.19 = f32[2,512,4096]{2,1,0:T(8,128)} fusion(bf16[512,2,128]{0,2,1:T(8,128)(2,1)S(1)} %bitcast.67, bf16[4096,256]{1,0:T(8,128)(2,1)S(1)} %copy-done.9), kind=kOutput, calls=%fused_computation.41 | convolution fusion | flops 1073741824 | bytes 19136512 | tf_op jit(solution)/shard_map/qhd,khd->hqk/dot_general | solution.py:88
  297.5 19.6 %fusion.16 = bf16[2,128,4096]{2,1,0:T(8,128)(2,1)} fusion(bf16[512,2,128]{0,2,1:T(8,128)(2,1)} %bitcast.88, bf16[2,512,4096]{2,1,0:T(8,128)(2,1)} %divide_convert_fusion, f32[2,512,4096]{2,1,0:T(8,128)} %fusion.19), kind=kOutput, calls=%fused_computation.33 | convolution fusion | flops 1104155648 | bytes 27525120 | tf_op jit(solution)/shard_map/hqk,qhd->khd/dot_general | solution.py:99
  317.1 4.0 pad_maximum_fusion.1
  321.2 5.0 convolution_convert_fusion.5
  326.3 20.8 %fusion.28 = bf16[2,128,512]{2,1,0:T(8,128)(2,1)} fusion(bf16[4096,2,128]{0,2,1:T(8,128)(2,1)S(1)} %bitcast.69, bf16[2,512,4096]{2,1,0:T(8,128)(2,1)} %divide_convert_fusion, f32[2,512,4096]{2,1,0:T(8,128)} %fusion.19), kind=kOutput, calls=%fused_computation.47 | convolution fusion | flops 1103238144 | bytes 27525120 | tf_op jit(solution)/shard_map/hqk,khd->qhd/dot_general | solution.py:95
  347.1 6.3 %fusion.75 = f32[512,4096]{1,0:T(8,128)} fusion(bf16[512,256]{0,1:T(8,128)(2,1)} %bitcast.73, bf16[4096,256]{1,0:T(8,128)(2,1)} %param.17), kind=kOutput, calls=%fused_computation.110 | convolution fusion | flops 1073741824 | bytes 10747904 | tf_op jit(solution)/shard_map/dot_general | solution.py:113
  360.4 4.4 add_convert_fusion
  365.1 3.8 convolution_convert_fusion.4
  371.9 9.5 %pad_maximum_fusion = bf16[4096,768]{0,1:T(8,128)(2,1)} fusion(bf16[4096,256]{0,1:T(8,128)(2,1)S(1)} %convolution_convert_fusion.2, bf16[4096,256]{0,1:T(8,128)(2,1)S(1)} %convolution_convert_fusion.3, bf16[4096,256]{0,1:T(8,128)(2,1)S(1)} %convolution_convert_fusion.4), kind=kLoop, calls=%fused_computation.28 | loop fusion | flops 18874368 | bytes 12582912 | tf_op jit(solution)/shard_map/concatenate | solution.py:148
  385.7 6.5 %scatter_custom_fusion = f32[2048,256]{1,0:T(8,128)} fusion(f32[2048,256]{1,0:T(8,128)} %convert_element_type.99, s32[512]{0:T(512)S(1)} %compare_select_fusion, bf16[512,256]{1,0:T(8,128)(2,1)S(1)} %copy-done.12, f32[512]{0:T(512)S(1)} %broadcast_select_fusion.2), kind=kCustom, calls=%fused_computation.58 | custom fusion | flops 393216 | bytes 2361344 | tf_op jit(solution)/shard_map/scatter-add | solution.py:73
  394.8 34.5 %psum.29 = f32[512]{0:T(512)S(1)} all-reduce(f32[512]{0:T(512)S(1)} %get-tuple-element.40), channel_id=1, replica_groups=mesh['ctx'=8,'tp'=16] {'tp'}, use_global_device_ids=true, to_apply=%region_10.12 | all-reduce | flops 512 | bytes 4096 | tf_op jit(solution)/shard_map/psum | solution.py:125
  431.1 69.5 %all-reduce.3.cloned.1.call-done = bf16[512,4096]{1,0:T(8,128)(2,1)} async-done(((bf16[512,4096]{1,0:T(8,128)(2,1)}), bf16[512,4096]{1,0:T(8,128)(2,1)}) %all-reduce.3.cloned.1.call-update) | async-done | bytes 4194320 | tf_op jit(solution)/shard_map/psum | solution.py:124
  500.7 6.6 %convert_element_type.122 = f32[512,4096]{1,0:T(8,128)} convert(bf16[512,4096]{1,0:T(8,128)(2,1)} %all-reduce.3.cloned.1.call-done) | non-fusion elementwise | flops 2097152 | bytes 12582912 | tf_op jit(solution)/shard_map/convert_element_type | solution.py:124
  508.8 7.2 %scatter_custom_fusion.1 = f32[2048,256]{1,0:T(8,128)} fusion(f32[2048,256]{1,0:T(8,128)} %convert_element_type.113, s32[512]{0:T(512)S(1)} %compare_select_fusion, f32[512,4096]{1,0:T(8,128)} %convert_element_type.122, s32[]{:T(128)} %constant.5.clone.1, s32[]{:T(128)S(6)} %select_n.32, f32[]{:T(128)} %constant.12.clone.1, ...), kind=kCustom, calls=%fused_computation.64 | custom fusion | flops 1310720 | bytes 2893828 | tf_op jit(solution)/shard_map/scatter-add | solution.py:139
  520.2 13.7 %all-reduce = (f32[256]{0:T(256)}, f32[256]{0:T(256)}) all-reduce(f32[256]{0:T(256)S(1)} %get-tuple-element.34, f32[256]{0:T(256)S(1)} %get-tuple-element.33), channel_id=1, replica_groups=mesh['ctx'=8,'tp'=16] {'ctx'}, use_global_device_ids=true, to_apply=%region_15.17 | all-reduce | flops 512 | bytes 4096 | tf_op jit(solution)/shard_map/psum | solution.py:138
  533.9 11.3 %reduce-scatter.9.cloned.1.call-done = bf16[512,768]{0,1:T(8,128)(2,1)} async-done(((bf16[4096,768]{0,1:T(8,128)(2,1)}), bf16[512,768]{0,1:T(8,128)(2,1)}) %reduce-scatter.9.cloned.1.call-update) | async-done | bytes 786448 | tf_op jit(solution)/shard_map/reduce_scatter | solution.py:147
  (97 shorter events, 54.6 us)
Async XLA Ops:
  7.2 133.9 %copy-start = (bf16[256,4096]{1,0:T(8,128)(2,1)S(1)}, bf16[256,4096]{1,0:T(8,128)(2,1)}, u32[]{:S(2)}) copy-start(bf16[256,4096]{1,0:T(8,128)(2,1)} %param.20) | copy-start | bytes 6291460
  7.2 65.6 %all-gather.8.cloned.1.call-start = ((), (), s32[]{:S(2)}) async-start(), calls=%async_computation.4 | async-start | bytes 4456448 | tf_op jit(solution)/shard_map/all_gather | solution.py:27
  12.5 94.3 %all-gather.12.cloned.1.call-start = ((), (), s32[]{:S(2)}) async-start(), calls=%async_computation.6 | async-start | bytes 2359296 | tf_op jit(solution)/shard_map/all_gather | solution.py:42
  72.8 3.4 copy-start.2
  79.9 53.6 %all-gather.10.cloned.1.call-start = ((), (), s32[]{:S(2)}) async-start(), calls=%async_computation.5 | async-start | bytes 2359296 | tf_op jit(solution)/shard_map/all_gather | solution.py:43
  102.1 118.4 %reduce-scatter.5.cloned.1.call-start = ((), (), s32[]{:S(2)}) async-start(), calls=%async_computation.7 | async-start | bytes 4456448 | tf_op jit(solution)/shard_map/reduce_scatter | solution.py:67
  106.9 15.6 %copy-start.17 = (bf16[512,256]{0,1:T(8,128)(2,1)}, bf16[512,256]{0,1:T(8,128)(2,1)S(1)}, u32[]{:S(2)}) copy-start(bf16[512,256]{0,1:T(8,128)(2,1)S(1)} %convolution_convert_fusion.8) | copy-start | bytes 786436
  140.4 0.7 copy-start.13
  141.1 3.3 copy-start.16
  141.1 3.3 copy-start.8
  144.3 136.7 %all-gather.14.cloned.1.call-start = ((), (), s32[]{:S(2)}) async-start(), calls=%async_computation.8 | async-start | bytes 4456448 | tf_op jit(solution)/shard_map/all_gather | solution.py:79
  222.5 133.8 %reduce-scatter.7.cloned.1.call-start = ((), (), s32[]{:S(2)}) async-start(), calls=%async_computation.9 | async-start | bytes 4718592 | tf_op jit(solution)/shard_map/reduce_scatter | solution.py:105
  284.5 4.8 copy-start.9
  321.1 5.1 copy-start.11
  321.2 108.2 %reduce-scatter.11.cloned.1.call-start = ((), (), s32[]{:S(2)}) async-start(), calls=%async_computation.12 | async-start | bytes 2359296 | tf_op jit(solution)/shard_map/reduce_scatter | solution.py:156
  326.2 174.5 %all-reduce.3.cloned.1.call-start = ((), (), s32[]{:S(2)}) async-start(), calls=%async_computation.10 | async-start | bytes 8388608 | tf_op jit(solution)/shard_map/psum | solution.py:124
  353.4 6.1 %copy-start.10 = (bf16[4096,256]{1,0:T(8,128)(2,1)S(1)}, bf16[4096,256]{1,0:T(8,128)(2,1)}, u32[]{:S(2)}) copy-start(bf16[4096,256]{1,0:T(8,128)(2,1)} %param.19) | copy-start | bytes 6291460
  356.3 4.1 copy-start.5
  364.8 180.4 %reduce-scatter.9.cloned.1.call-start = ((), (), s32[]{:S(2)}) async-start(), calls=%async_computation.11 | async-start | bytes 7077888 | tf_op jit(solution)/shard_map/reduce_scatter | solution.py:147
  365.0 3.8 copy-start.3
  365.0 3.8 copy-start.14
  381.4 0.7 copy-start.15
  381.4 1.3 copy-start.7
  382.0 3.6 copy-start.12
  500.7 6.7 %copy-start.4 = (bf16[512,4096]{1,0:T(8,128)(2,1)S(1)}, bf16[512,4096]{1,0:T(8,128)(2,1)}, u32[]{:S(2)}) copy-start(bf16[512,4096]{1,0:T(8,128)(2,1)} %all-gather.8.cloned.1.call-done) | copy-start | bytes 12582916
  500.7 6.7 %copy-start.6 = (bf16[512,4096]{1,0:T(8,128)(2,1)S(1)}, bf16[512,4096]{1,0:T(8,128)(2,1)}, u32[]{:S(2)}) copy-start(bf16[512,4096]{1,0:T(8,128)(2,1)} %all-reduce.3.cloned.1.call-done) | copy-start | bytes 12582916
  516.1 35.3 %copy-start.1 = (bf16[256,4096]{1,0:T(8,128)(2,1)S(1)}, bf16[256,4096]{1,0:T(8,128)(2,1)}, u32[]{:S(2)}) copy-start(bf16[256,4096]{1,0:T(8,128)(2,1)} %param.20) | copy-start | bytes 6291460
Sparse Core Ops, SparseCore 0:
  12.7 60.1 all-gather.7
  80.0 25.6 all-gather.11
  108.0 25.4 all-gather.9
  144.5 76.0 reduce-scatter.4
  223.3 57.6 all-gather.13
  321.3 34.9 reduce-scatter.6
  358.8 32.5 reduce-scatter.10
  395.2 105.4 all-reduce.2
  503.2 41.9 reduce-scatter.8
where the time goes:
time: 564 us; the launch traced here: 558 us
  waiting for transfers between devices  234 us (41%)
  matrix products  120 us (21%)
  blocking collectives  100 us (18%)
  other arithmetic  67.3 us (12%)
  local copies, waits for them, and re-layouts  19.6 us (3%)
  between operations  15 us (3%)
    psum x1, waiting for transfers between devices, body(): lax.psum(norm_part.astype(jnp.bfloat16), 'tp').astype(jnp.float32)  69.5 us
    all_gather x1, waiting for transfers between devices, body(): shard_piece = lax.all_gather(block_grad, 'tp', axis=1, tiled=True)  58.1 us
    reduce_scatter x1, waiting for transfers between devices, body(): lax.psum_scatter(partial_out.astype(jnp.bfloat16), 'tp', scatter_dimensio...  51.4 us
    all_gather x1, waiting for transfers between devices, body(): lax.all_gather(mine_rows, 'tp', axis=1, tiled=True)  39.4 us
    psum x1, blocking collectives, body(): gate_dot = lax.psum(gate_part, 'tp')  34.5 us
    dot_general x1, matrix products, body(): jnp.einsum('hqk,khd->qhd', score_grad, key_heads, preferred_element_type=...  20.8 us
    all_gather x1, blocking collectives, body(): lax.all_gather(norm_gain, 'tp', axis=0, tiled=True)  20.1 us
    dot_general x1, matrix products, body(): jnp.einsum('hqk,qhd->khd', score_grad, query_heads, preferred_element_typ...  19.6 us
  transfers between devices with their start and end apart: 9, of which 7 were waited for; matrix products, arithmetic and copies ran while one was open for 24% of the time, Pallas kernels for 0%

commit v1 on v0

v1 whole, which is shorter than its diff:
```python
import math

import jax
import jax.numpy as jnp
from jax import lax
from jax.experimental import pallas as pl
from jax.experimental.pallas import tpu as pltpu
from jax.sharding import PartitionSpec as P

D = 4096
HD = 128
CAP = 512
F32 = jnp.float32
BF16 = jnp.bfloat16
MESH_ID = pl.DeviceIdType.MESH
SCALING = HD ** (-0.5)
EXP2_SCALE = SCALING * math.log2(math.e)
FAR = -1e30
LAST_LAST = (((1,), (1,)), ((), ()))
FIRST_FIRST = (((0,), (0,)), ((), ()))
HOPS = (2, 1, -1, 0)


def pick(i, values):
    out = values[-1]
    for k in range(len(values) - 2, -1, -1):
        out = jnp.where(i == k, values[k], out)
    return out


def steps(count, work, after):
    @pl.loop(0, count)
    def _(i):
        work(i)
        for k, acts in after.items():

            @pl.when(i == k)
            def _():
                for act, *arguments in acts:
                    act(*arguments)


def dot(a, b, dims=(((1,), (0,)), ((), ()))):
    return lax.dot_general(a, b, dims, preferred_element_type=F32)


class Place:
    def __init__(self):
        self.ctx = lax.axis_index("ctx")
        self.tp = lax.axis_index("tp")
        self.x, self.core = lax.div(self.ctx, 2), lax.rem(self.ctx, 2)
        self.y, self.z = lax.div(self.tp, 4), lax.rem(self.tp, 4)

    def tp_at(self, dy, dz):
        return lax.rem(self.y + dy + 4, 4) * 4 + lax.rem(self.z + dz + 4, 4)

    def ctx_at(self, dx, other=0):
        return lax.rem(self.x + dx + 4, 4) * 2 + lax.rem(self.core + other, 2)

    def near(self, axis, step):
        if axis == "y":
            return (self.ctx, self.tp_at(step, 0))
        if axis == "z":
            return (self.ctx, self.tp_at(0, step))
        if axis == "x":
            return (self.ctx_at(step), self.tp)
        return (self.ctx_at(0, 1), self.tp)

    def tp_peer(self, p):
        return (self.ctx, lax.rem(self.tp + p, 16))

    def ctx_peer(self, p):
        return (lax.rem(self.ctx + p, 8), self.tp)


def greet(partners):
    barrier = pltpu.get_barrier_semaphore()
    for partner in partners:
        pl.semaphore_signal(barrier, inc=1, device_id=partner, device_id_type=MESH_ID)


def meet(partners):
    pl.semaphore_wait(pltpu.get_barrier_semaphore(), len(partners))


def remote(src, dst, sems, at, where):
    return pltpu.make_async_remote_copy(
        src_ref=src,
        dst_ref=dst,
        send_sem=sems.at[0, at],
        recv_sem=sems.at[1, at],
        device_id=where,
        device_id_type=MESH_ID,
    )


def add_into(dst, *terms):
    rows = dst.shape[0]
    slab = min(rows, 128 if dst.shape[1] <= 1024 else 16)

    @pl.loop(0, rows // slab)
    def _(i):
        at = pl.ds(pl.multiple_of(i * slab, slab), slab)
        if len(terms) == 1:
            dst[at] = dst[at] + terms[0][at]
        else:
            total = dst[at].astype(F32)
            for term in terms:
                total = total + term[at].astype(F32)
            dst[at] = total.astype(dst.dtype)


def sum_to(out, *terms):
    rows = out.shape[0]
    slab = min(rows, 128 if out.shape[1] <= 1024 else 16)

    @pl.loop(0, rows // slab)
    def _(i):
        at = pl.ds(pl.multiple_of(i * slab, slab), slab)
        total = terms[0][at].astype(F32)
        for term in terms[1:]:
            total = total + term[at].astype(F32)
        out[at] = total.astype(out.dtype)


def torus_block(place, half, a, b):
    return place.tp_at(b, a) if half == 0 else place.tp_at(a, b)


class TorusGather:
    def __init__(self, place, buf, sems):
        self.place, self.buf, self.sems = place, buf, sems
        self.rows = buf.shape[2]

    def plan(self, half, number):
        axes = ("z", "y") if half == 0 else ("y", "z")
        if number < 4:
            a, b, step, part = ((0, 0, 1, None), (0, 0, -1, None), (-1, 0, 1, 0), (1, 0, -1, 1))[number]
            axis = axes[0]
        else:
            a = (0, -1, 1, 2)[(number - 4) // 4]
            b, step, part = ((0, 1, None), (0, -1, None), (-1, 1, 0), (1, -1, 1))[(number - 4) % 4]
            axis = axes[1]
        ref = self.buf.at[torus_block(self.place, half, a, b), half]
        if part is not None:
            ref = ref.at[pl.ds(part * (self.rows // 2), self.rows // 2)]
        return remote(ref, ref, self.sems, half * 20 + number, self.place.near(axis, step))

    def start(self, *numbers):
        for number in numbers:
            for half in (0, 1):
                self.plan(half, number).start()

    def arrive(self, *numbers):
        for number in numbers:
            for half in (0, 1):
                self.plan(half, number).wait_recv()

    def pass_on(self, *pairs):
        for come, go in pairs:
            for half in (0, 1):
                self.plan(half, come).wait_recv()
                self.plan(half, go).start()

    def stage0(self):
        self.start(0, 1, 4, 5)

    def stage1(self):
        self.pass_on((0, 2), (1, 3))
        self.start(8, 9, 12, 13)

    def stage2(self):
        self.pass_on((4, 6), (5, 7))

    def stage3(self):
        self.arrive(2, 3)
        self.start(16, 17)

    def stage4(self):
        self.pass_on((8, 10), (9, 11), (12, 14), (13, 15))

    def stage5(self):
        self.pass_on((16, 18), (17, 19))

    def stage6(self):
        self.arrive(6, 7, 10, 11, 14, 15, 18, 19)

    def finish(self):
        for number in range(20):
            for half in (0, 1):
                self.plan(half, number).wait_send()


class TorusScatter:
    def __init__(self, place, part, small, big, sems):
        self.place, self.part, self.small, self.big, self.sems = place, part, small, big, sems

    def term(self, half, i, b):
        a, c = (HOPS[i], b) if i < 4 else (b, 0)
        return self.part.at[torus_block(self.place, half, a, c), half]

    def plan(self, half, i, k):
        axes = ("z", "y") if half == 0 else ("y", "z")
        axis = axes[1] if i < 4 else axes[0]
        step = 1 if k % 2 == 0 else -1
        if k < 2:
            src = self.term(half, i, 2)
            rows = src.shape[0] // 2
            src = src.at[pl.ds(k * rows, rows)]
            dst = self.small.at[half, i, k]
        else:
            src = self.term(half, i, step)
            dst = self.big.at[half, i, k - 2]
        return remote(src, dst, self.sems, half * 20 + i * 4 + k, self.place.near(axis, step))

    def far(self, *rounds):
        for i in rounds:
            for half in (0, 1):
                self.plan(half, i, 0).start()
                self.plan(half, i, 1).start()

    def middle(self, *rounds):
        for i in rounds:
            for half in (0, 1):
                for k, step in ((0, 1), (1, -1)):
                    self.plan(half, i, k).wait_recv()
                    term = self.term(half, i, step)
                    rows = term.shape[0] // 2
                    add_into(term.at[pl.ds(k * rows, rows)], self.small.at[half, i, k])
                    self.plan(half, i, 2 + k).start()

    def near(self, *rounds):
        for i in rounds:
            for half in (0, 1):
                self.plan(half, i, 2).wait_recv()
                self.plan(half, i, 3).wait_recv()
                add_into(self.term(half, i, 0), self.big.at[half, i, 0], self.big.at[half, i, 1])

    def last(self, out):
        for half in (0, 1):
            self.plan(half, 4, 2).wait_recv()
            self.plan(half, 4, 3).wait_recv()
            rows = self.part.shape[2]
            sum_to(
                out.at[pl.ds(half * rows, rows)],
                self.term(half, 4, 0), self.big.at[half, 4, 0], self.big.at[half, 4, 1],
            )

    def finish(self):
        for i in range(5):
            for half in (0, 1):
                for k in range(4):
                    self.plan(half, i, k).wait_send()


class ContextGather:
    def __init__(self, place, buf, cut, sems):
        self.place, self.buf, self.cut, self.sems = place, buf, cut, sems

    def plan(self, k):
        hop, axis, step, part = (
            (0, "core", 0, None), (0, "x", 1, None), (0, "x", -1, None),
            (-1, "x", 1, 0), (1, "x", -1, 1),
            (-1, "core", 0, None), (1, "core", 0, None), (2, "core", 0, None),
        )[k]
        ref = self.buf.at[self.place.ctx_at(hop)]
        if part is not None:
            ref = ref.at[pl.ds(0, self.cut) if part == 0 else pl.ds(self.cut, ref.shape[0] - self.cut)]
        return remote(ref, ref, self.sems, k, self.place.near(axis, step))

    def start(self, *numbers):
        for k in numbers:
            self.plan(k).start()

    def arrive(self, *numbers):
        for k in numbers:
            self.plan(k).wait_recv()

    def finish(self):
        for k in range(8):
            self.plan(k).wait_send()


class ContextScatter:
    def __init__(self, place, part, sib, small, big, sems):
        self.place, self.part, self.sib, self.small, self.big, self.sems = (
            place, part, sib, small, big, sems
        )

    def plan(self, k):
        place = self.place
        if k < 4:
            return self.sibling(k)
        step = 1 if k % 2 == 0 else -1
        if k < 6:
            src = self.part.at[place.ctx_at(2)]
            rows = src.shape[0] // 2
            src = src.at[pl.ds((k - 4) * rows, rows)]
            dst = self.small.at[k - 4]
        else:
            src = self.part.at[place.ctx_at(step)]
            dst = self.big.at[k - 6]
        return remote(src, dst, self.sems, k, place.near("x", step))

    def sibling(self, k):
        src = self.part.at[self.place.ctx_at(pick(k, HOPS), 1)]
        return remote(src, self.sib.at[k], self.sems, k, self.place.near("core", 0))

    def give(self, *hops):
        for k in hops:
            self.sibling(k).start()

    def take(self, *hops):
        for k in hops:
            self.sibling(k).wait_recv()
            add_into(self.part.at[self.place.ctx_at(pick(k, HOPS))], self.sib.at[k])

    def take_all(self):
        @pl.loop(0, 4)
        def _(k):
            self.take(k)

    def far(self):
        self.plan(4).start()
        self.plan(5).start()

    def near(self, *sides):
        for side in sides:
            k, step = ((4, 1), (5, -1))[side]
            self.plan(k).wait_recv()
            term = self.part.at[self.place.ctx_at(step)]
            rows = term.shape[0] // 2
            add_into(term.at[pl.ds((k - 4) * rows, rows)], self.small.at[k - 4])
            self.plan(k + 2).start()

    def last(self, out):
        self.plan(6).wait_recv()
        self.plan(7).wait_recv()
        sum_to(out, self.part.at[self.place.ctx_at(0)], self.big.at[0], self.big.at[1])

    def finish(self):
        for k in range(8):
            self.plan(k).wait_send()


class Exchange:
    def __init__(self, me, peer, count, buf, sems):
        self.me, self.peer, self.count, self.buf, self.sems = me, peer, count, buf, sems

    def plan(self, p):
        ref = self.buf.at[self.me]
        return remote(ref, ref, self.sems, p - 1, self.peer(p))

    def start(self):
        for p in range(1, self.count):
            self.plan(p).start()

    def total(self):
        for p in range(1, self.count):
            self.plan(p).wait_recv()
        return jnp.sum(self.buf[...], axis=0)

    def finish(self):
        for p in range(1, self.count):
            self.plan(p).wait_send()


def to_packed(first, second):
    lane = lax.broadcasted_iota(jnp.int32, (CAP, 128), 1)
    both = jnp.where(lane % 2 == 0, first, second).T
    return jnp.concatenate([pack(both[0:1]), pack(both[1:2])], axis=0)


def to_columns(rows):
    return jnp.concatenate([rows] * 16, axis=0).T


def pack(row):
    return jnp.concatenate([row[:, 128 * i : 128 * (i + 1)] for i in range(4)], axis=0)


def unpack(lines):
    row = jnp.concatenate([lines[i : i + 1] for i in range(4)], axis=1)
    return jnp.broadcast_to(row, (8, CAP))


SPOT_HOPS = (2, 2, 1, -1, 1, -1, 0, 0)
SPOT_CORES = (1, 0, 1, 1, 0, 0, 1, 0)


class Refs:
    pass


def gather_rows(r, staged, picked_columns, out):
    def chunk(i):
        token = lax.broadcasted_iota(jnp.int32, (CAP, CAP), 1) + i * CAP
        hit = jnp.where(picked_columns == token.astype(F32), 1.0, 0.0).astype(BF16)
        return dot(hit, r.part[staged + i].reshape(CAP, 256))

    out[...] = ((chunk(0) + chunk(1)) + (chunk(2) + chunk(3))).astype(BF16).reshape(2, 256, 256)


def scatter_rows(r, staged, goal, rows, hbm, sems, first):
    slot = lax.broadcasted_iota(jnp.int32, (1, CAP), 1)
    picked = jnp.where(slot < r.counts[0], r.picked[...].reshape(1, CAP), -1)

    @pl.loop(0, 4)
    def _(i):
        for half in range(2):
            if first:
                token = lax.broadcasted_iota(jnp.int32, (256, CAP), 0) + (i * CAP + half * 256)
                hit = jnp.where(picked == token, 1.0, 0.0)
                r.kv[2 * i + half, 0:256] = hit.astype(BF16)
                any_hit = jnp.max(hit, axis=1, keepdims=True) > 0.0
                for base in (staged + i, 4 + i):
                    old = r.bgrad[base, half].astype(F32)
                    r.bgrad[base, half] = jnp.where(any_hit, 0.0, old).astype(BF16)
            new = dot(r.kv[2 * i + half, 0:256], rows[...])
            r.bgrad[goal + i, half] = (r.bgrad[staged + i, half].astype(F32) + new).astype(BF16)
        pltpu.make_async_copy(r.bgrad.at[goal + i], hbm.at[i], sems.at[i]).start()


def forward_phase(place, r, partners):
    tp, ctx = place.tp, place.ctx
    picked_row = jnp.broadcast_to(r.picked[...].reshape(1, CAP).astype(F32), (8, CAP))
    picked_columns = to_columns(picked_row)[:, 0:1]
    r.stage_loads[0].wait()
    gather_rows(r, 0, picked_columns, r.rows)
    rows3 = r.rows[...].astype(F32).reshape(CAP, 256)
    gain = r.gain[...].astype(F32).reshape(1, 256)
    router = r.router[...].astype(F32).reshape(1, 256)
    r.normed[tp] = (rows3 * gain).astype(BF16).reshape(2, 256, 256)
    meet(partners)
    rows_in = TorusGather(place, r.normed, r.normed_sems)
    rows_in.stage0()

    stats = Exchange(tp, place.tp_peer, 16, r.stat_buf, r.stat_sems)
    squares = jnp.sum(rows3 * rows3, axis=1, keepdims=True)
    logits = jnp.sum(rows3 * router, axis=1, keepdims=True)
    r.stat_buf[tp] = to_packed(squares, logits)
    stats.start()
    r.stage_loads[1].wait()
    gather_rows(r, 4, picked_columns, r.uprows)
    r.bgrad[tp] = r.uprows[...]
    r.grads_in = grads_in = TorusGather(place, r.bgrad, r.bgrad_sems)

    def project(i):
        b = pick(i, (0, -1, 1, 2))
        for half in (0, 1):
            rows = pl.ds(half * 256, 256)
            terms = []
            for a in range(4):
                t = torus_block(place, half, a, b)
                terms.append(dot(r.normed[t, half], r.w_in[t]))
            term = (terms[0] + terms[1]) + (terms[2] + terms[3])
            r.acc[rows] = jnp.where(i == 0, term, r.acc[rows] + term)

    rows_in.stage1()
    rows_in.stage2()
    rows_in.stage3()
    for load in r.loads:
        load.wait()
    steps(
        4, project,
        {0: [(rows_in.stage4,), (rows_in.stage5,), (grads_in.stage0,)], 2: [(rows_in.stage6,)]},
    )
    total = stats.total()
    inverse = lax.rsqrt(to_columns(unpack(total[0:4]))[:, 0:1] * (1.0 / D) + 1e-05)
    gate = jax.nn.sigmoid(to_columns(unpack(total[4:8]))[:, 0:1])
    slot = lax.broadcasted_iota(jnp.int32, (CAP, 1), 0)
    r.inverse[...] = jnp.broadcast_to(inverse, (CAP, 128))
    r.gate[...] = jnp.broadcast_to(gate, (CAP, 128))
    r.live_gate[...] = jnp.broadcast_to(jnp.where(slot < r.counts[0], gate, 0.0), (CAP, 128))
    r.kv[ctx, pl.ds(0, CAP)] = (r.acc[:, 256:768] * inverse).astype(BF16)
    count = r.counts[0]
    high = lax.div(count, 256) * 256
    line = lax.broadcasted_iota(jnp.int32, (16, CAP), 0)
    r.kv[ctx, pl.ds(CAP, 16)] = jnp.where(
        line == 0, high.astype(F32), jnp.where(line == 1, (count - high).astype(F32), 0.0)
    ).astype(BF16)
    keys_in = ContextGather(place, r.kv, 272, r.kv_sems)
    keys_in.start(0, 1, 2)
    r.q[...] = (r.acc[:, 0:256] * inverse).astype(BF16)
    grads_in.stage1()

    for head in range(2):
        r.high[head] = jnp.full((8, CAP), FAR, F32)
        r.mass[head] = jnp.zeros((8, CAP), F32)
        r.out_t[head] = jnp.zeros((HD, CAP), F32)

    def attend(c):
        marks = r.kv[c, pl.ds(CAP, 16)].astype(F32)
        query = lax.broadcasted_iota(jnp.int32, (1, CAP), 1) + ((ctx - c) * CAP + 1)
        limit = jnp.minimum(marks[0:1] + marks[1:2], query.astype(F32))
        allowed = lax.broadcasted_iota(jnp.int32, (CAP, CAP), 0).astype(F32) < limit
        for head in range(2):
            keys = r.kv[c, 0:CAP, head * HD : (head + 1) * HD]
            values = r.kv[c, 0:CAP, 256 + head * HD : 256 + (head + 1) * HD]
            scores = dot(keys, r.q[:, head * HD : (head + 1) * HD], LAST_LAST)
            scores = jnp.where(allowed, scores, FAR)
            before = r.high[head][0:1]
            high = jnp.maximum(before, jnp.max(scores, axis=0, keepdims=True))
            fade = jnp.exp2((before - high) * EXP2_SCALE)
            lifted = jnp.exp2((scores - high) * EXP2_SCALE)
            r.high[head] = jnp.broadcast_to(high, (8, CAP))
            mass = r.mass[head][0:1] * fade + jnp.sum(lifted, axis=0, keepdims=True)
            r.mass[head] = jnp.broadcast_to(mass, (8, CAP))
            r.out_t[head] = r.out_t[head] * fade + dot(values, lifted.astype(BF16), FIRST_FIRST)

    def attend_step(i):
        c = place.ctx_at(pick(i, (0, 0, -1, 1, -1, 1, 2, 2)), pick(i, (0, 1, 0, 0, 1, 1, 0, 1)))

        @pl.when(c <= ctx)
        def _():
            attend(c)

    steps(
        8, attend_step,
        {
            0: [(grads_in.stage2,), (grads_in.stage3,), (keys_in.arrive, 0)],
            1: [
                (grads_in.stage4,),
                (keys_in.arrive, 1), (keys_in.start, 3, 5),
                (keys_in.arrive, 2), (keys_in.start, 4, 6),
            ],
            3: [(grads_in.stage5,), (keys_in.arrive, 5, 6)],
            4: [(keys_in.arrive, 3, 4), (keys_in.start, 7)],
            6: [(keys_in.arrive, 7)],
        },
    )
    for head in range(2):
        out = (r.out_t[head] * (1.0 / r.mass[head][0:1])).T
        r.attended[:, head * HD : (head + 1) * HD] = out.astype(BF16)
    rows_in.finish()
    stats.finish()
    keys_in.finish()


def backward_phase(place, r):
    tp, ctx = place.tp, place.ctx
    out_sum = TorusScatter(place, r.part, r.out_small, r.out_big, r.out_sems)

    def project_out(i):
        b = pick(i, (2, 1, -1, 0))
        for half in (0, 1):
            for a in range(4):
                t = torus_block(place, half, a, b)
                cols = pl.ds(pl.multiple_of(t * 256, 256), 256)
                r.part[t, half] = dot(
                    r.attended[half * 256 : (half + 1) * 256], r.w_out[:, cols]
                ).astype(BF16)

    steps(4, project_out, {0: [(out_sum.far, 0, 1, 2, 3)]})
    r.grads_in.stage6()

    live_gate = r.live_gate[:, 0:1]
    r.grads[:, 0:256] = (r.attended[...].astype(F32) * live_gate).astype(BF16)
    r.acc[:, 0:256] = jnp.zeros((CAP, 256), F32)

    @pl.loop(0, 16, unroll=4)
    def _(t):
        cols = pl.ds(pl.multiple_of(t * 256, 256), 256)
        piece = r.bgrad[t].reshape(CAP, 256)
        r.acc[:, 0:256] += dot(piece, r.w_out[:, cols], LAST_LAST)
        term = dot(r.grads[:, 0:256], piece, FIRST_FIRST)
        r.wo_part[:, :, cols] = term.astype(BF16).reshape(8, 32, 256)

    wo_sum = ContextScatter(place, r.wo_part, r.wo_sib, r.wo_small, r.wo_big, r.wo_sems)
    wo_sum.give(0, 1, 2, 3)
    r.agrad[...] = (r.acc[:, 0:256] * live_gate).astype(BF16)
    r.grads_in.finish()
    for load in r.base_loads:
        load.start()
    for head in range(2):
        cols = slice(head * HD, (head + 1) * HD)
        product = r.agrad[:, cols].astype(F32) * r.attended[:, cols].astype(F32)
        r.spread[head] = jnp.broadcast_to(jnp.sum(product.T, axis=0, keepdims=True), (8, CAP))
        r.high[head] = r.high[head] * EXP2_SCALE + jnp.log2(r.mass[head])
        r.out_t[head] = jnp.zeros((HD, CAP), F32)

    def attend_back(c):
        marks = r.kv[c, pl.ds(CAP, 16)].astype(F32)
        query = lax.broadcasted_iota(jnp.int32, (1, CAP), 1) + ((ctx - c) * CAP + 1)
        limit = jnp.minimum(marks[0:1] + marks[1:2], query.astype(F32))
        allowed = lax.broadcasted_iota(jnp.int32, (CAP, CAP), 0).astype(F32) < limit
        for head in range(2):
            cols = slice(head * HD, (head + 1) * HD)
            keys = r.kv[c, 0:CAP, head * HD : (head + 1) * HD]
            values = r.kv[c, 0:CAP, 256 + head * HD : 256 + (head + 1) * HD]
            queries, grads = r.q[:, cols], r.agrad[:, cols]
            scores = dot(keys, queries, LAST_LAST)
            scores = jnp.where(allowed, scores, FAR)
            probs = jnp.exp2(scores * EXP2_SCALE - r.high[head][0:1])
            prob_grad = dot(values, grads, LAST_LAST)
            score_grad = (probs * (prob_grad - r.spread[head][0:1])).astype(BF16)
            r.kv_part[c, :, 256 + head * HD : 256 + (head + 1) * HD] = dot(
                probs.astype(BF16), grads
            ).astype(BF16)
            r.kv_part[c, :, head * HD : (head + 1) * HD] = (
                dot(score_grad, queries) * SCALING
            ).astype(BF16)
            r.out_t[head] = r.out_t[head] + dot(keys, score_grad, FIRST_FIRST)

    def back_step(i):
        c = place.ctx_at(pick(i, SPOT_HOPS), pick(i, SPOT_CORES))

        @pl.when(c <= ctx)
        def _():
            attend_back(c)

        @pl.when(c > ctx)
        def _():
            r.kv_part[c] = jnp.zeros((CAP, CAP), BF16)

    kv_sum = ContextScatter(place, r.kv_part, r.kv_sib, r.kv_small, r.kv_big, r.kv_grad_sems)
    steps(
        8, back_step,
        {
            0: [(kv_sum.give, 0), (out_sum.middle, 0, 1, 2, 3)],
            1: [(kv_sum.take, 0), (kv_sum.far,)],
            2: [(kv_sum.give, 1), (wo_sum.take_all,), (wo_sum.far,)],
            3: [(kv_sum.give, 2)],
            4: [(kv_sum.take, 1), (kv_sum.near, 0)],
            5: [(kv_sum.take, 2), (kv_sum.near, 1), (wo_sum.near, 0, 1)],
            6: [(kv_sum.give, 3), (out_sum.near, 0), (out_sum.far, 4)],
            7: [(out_sum.near, 1, 2), (out_sum.middle, 4)],
        },
    )
    for head in range(2):
        r.grads[:, head * HD : (head + 1) * HD] = (r.out_t[head] * SCALING).T.astype(BF16)
    kv_sum.take(3)
    out_sum.near(3)

    def weight_term(part, lower, upper, c):
        pair = [r.normed[c * 2 + i].reshape(CAP, 256) for i in range(2)]
        term = dot(jnp.concatenate(pair, axis=1), r.scaled[:, lower:upper], FIRST_FIRST)
        part[c] = term.astype(BF16)

    inverse = r.inverse[:, 0:1]
    r.scaled[:, 0:256] = (r.grads[:, 0:256].astype(F32) * inverse).astype(BF16)
    wq_sum = ContextScatter(place, r.wq_part, r.wq_sib, r.wq_small, r.wq_big, r.wq_sems)

    def query_step(i):
        weight_term(r.wq_part, 0, 256, place.ctx_at(pick(lax.rem(i, 4), HOPS), 1 - lax.div(i, 4)))

        @pl.when(i < 4)
        def _():
            wq_sum.give(i)

    steps(8, query_step, {})
    wq_sum.take_all()
    wq_sum.far()

    out_sum.last(r.wide)
    block_out = r.wide[...]
    rows3 = r.rows[...].astype(F32).reshape(CAP, 256)
    chosen_grad = r.uprows[...].astype(F32).reshape(CAP, 256)
    r.mixed_rows[...] = (rows3 + live_gate * block_out).astype(BF16)
    gates = Exchange(tp, place.tp_peer, 16, r.gate_buf, r.gate_sems)
    gate_part = jnp.sum(chosen_grad * block_out, axis=1, keepdims=True)
    r.gate_buf[tp] = to_packed(gate_part, gate_part)
    gates.start()

    kv_sum.last(r.grads.at[:, pl.ds(256, 512)])
    r.scaled[:, 256:768] = (r.grads[:, 256:768].astype(F32) * inverse).astype(BF16)
    out_sum.finish()
    kv_sum.finish()
    norm_sum = TorusScatter(place, r.part, r.norm_small, r.norm_big, r.norm_sems)

    def project_back(i):
        b = pick(i, (2, 1, -1, 0))
        for half in (0, 1):
            for a in range(4):
                t = torus_block(place, half, a, b)
                r.part[t, half] = dot(
                    r.grads[half * 256 : (half + 1) * 256], r.w_in[t], LAST_LAST
                ).astype(BF16)

    steps(4, project_back, {0: [(norm_sum.far, 0, 1, 2, 3)], 2: [(wq_sum.near, 0, 1)]})

    dot_part = jnp.sum(r.grads[:, 0:256].astype(F32) * r.q[...].astype(F32), axis=1, keepdims=True)
    dot_part = dot_part + jnp.sum(
        r.grads[:, 256:768].astype(F32) * r.kv[ctx, 0:CAP, :].astype(F32), axis=1, keepdims=True
    )
    dot_part = dot_part / inverse
    dots = Exchange(tp, place.tp_peer, 16, r.dot_buf, r.dot_sems)
    r.dot_buf[tp] = to_packed(dot_part, dot_part)
    dots.start()
    wkv_sum = ContextScatter(place, r.kv_part, r.wkv_sib, r.wkv_small, r.wkv_big, r.wkv_sems)

    def key_value_step(i):
        c = place.ctx_at(pick(i, SPOT_HOPS), pick(i, SPOT_CORES))
        weight_term(r.kv_part, 256, 768, c)

    steps(
        8, key_value_step,
        {
            0: [(wkv_sum.give, 0), (norm_sum.middle, 0, 1, 2, 3)],
            1: [(wkv_sum.take, 0), (wkv_sum.far,)],
            2: [(wkv_sum.give, 1)],
            3: [(wkv_sum.give, 2)],
            4: [(wkv_sum.take, 1), (wkv_sum.near, 0)],
            5: [(wkv_sum.take, 2), (wkv_sum.near, 1), (norm_sum.near, 0), (norm_sum.far, 4)],
            6: [(wkv_sum.give, 3)],
        },
    )
    for load in r.base_loads:
        load.wait()
    scatter_rows(r, 0, 8, r.mixed_rows, r.o_mixed, r.mixed_sems, True)
    norm_sum.near(1, 2)
    norm_sum.middle(4)
    wkv_sum.take(3)
    norm_sum.near(3)
    wo_sum.last(r.grad_out)
    r.out_copy("grad_out", r.grad_out, r.o_grad_out)
    wq_sum.last(r.grad_q)
    r.out_copy("grad_q", r.grad_q, r.o_grad_q)

    gate_dot = to_columns(unpack(gates.total()[0:4]))[:, 0:1]
    row_dot = to_columns(unpack(dots.total()[0:4]))[:, 0:1]
    slot = lax.broadcasted_iota(jnp.int32, (CAP, 1), 0)
    alive = slot < r.counts[0]
    gate = r.gate[:, 0:1]
    gate_grad = jnp.where(alive, gate_dot * gate * (1.0 - gate), 0.0)
    router_part = jnp.sum(gate_grad * rows3, axis=0, keepdims=True)
    gain = r.gain[...].astype(F32).reshape(1, 256)
    router = r.router[...].astype(F32).reshape(1, 256)
    known = gate_grad * router - rows3 * (inverse * inverse * inverse * row_dot * (1.0 / D))
    norm_sum.last(r.wide)
    normed_grad = r.wide[...]
    sums = Exchange(ctx, place.ctx_peer, 8, r.sum_buf, r.sum_sems)
    gain_part = jnp.sum(normed_grad * rows3 * inverse, axis=0, keepdims=True)
    line = lax.broadcasted_iota(jnp.int32, (8, 256), 0)
    r.sum_buf[ctx] = jnp.where(line == 0, gain_part, router_part)
    sums.start()
    rows_grad = jnp.where(alive, inverse * (normed_grad * gain) + known, 0.0)
    r.grad_rows[...] = (chosen_grad + rows_grad).astype(BF16)
    scatter_rows(r, 4, 12, r.grad_rows, r.o_grad_states, r.states_sems, False)
    wkv_sum.last(r.grad_kv)
    r.out_copy("grad_k", r.acc.at[:, pl.ds(256, 256)], r.o_grad_k)
    r.out_copy("grad_v", r.acc.at[:, pl.ds(512, 256)], r.o_grad_v)
    r.o_small[...] = sums.total()
    for each in (wo_sum, wq_sum, wkv_sum, norm_sum, gates, dots, sums):
        each.finish()


DMA = pltpu.SemaphoreType.DMA


def vm(shape, dtype):
    return pltpu.VMEM(shape, dtype)


def scatter_scratch(name, rows, cols):
    return {
        name + "_part": vm((8, rows, cols), BF16),
        name + "_sib": vm((4, rows, cols), BF16),
        name + "_small": vm((2, rows // 2, cols), BF16),
        name + "_big": vm((2, rows, cols), BF16),
    }


def scratch_table():
    table = {
        "normed": vm((16, 2, 256, 256), BF16),
        "bgrad": vm((16, 2, 256, 256), BF16),
        "part": vm((16, 2, 256, 256), BF16),
        "kv": vm((8, CAP + 16, CAP), BF16),
        "w_in": vm((16, 256, 768), BF16),
        "w_out": vm((256, D), BF16),
        "acc": vm((CAP, 768), F32),
        "wide": vm((CAP, 256), F32),
        "q": vm((CAP, 256), BF16),
        "attended": vm((CAP, 256), BF16),
        "agrad": vm((CAP, 256), BF16),
        "grads": vm((CAP, 768), BF16),
        "high": vm((2, 8, CAP), F32),
        "mass": vm((2, 8, CAP), F32),
        "spread": vm((2, 8, CAP), F32),
        "out_t": vm((2, HD, CAP), F32),
        "inverse": vm((CAP, 128), F32),
        "live_gate": vm((CAP, 128), F32),
        "gate": vm((CAP, 128), F32),
        "stat_buf": vm((16, 8, 128), F32),
        "gate_buf": vm((16, 8, 128), F32),
        "dot_buf": vm((16, 8, 128), F32),
        "sum_buf": vm((8, 8, 256), F32),
        "out_small": vm((2, 5, 2, 128, 256), BF16),
        "out_big": vm((2, 5, 2, 256, 256), BF16),
        "norm_small": vm((2, 5, 2, 128, 256), BF16),
        "norm_big": vm((2, 5, 2, 256, 256), BF16),
        "rows": vm((2, 256, 256), BF16),
        "uprows": vm((2, 256, 256), BF16),
        "scaled": vm((CAP, 768), BF16),
        "mixed_rows": vm((CAP, 256), BF16),
        "grad_rows": vm((CAP, 256), BF16),
        "grad_out": vm((32, D), F32),
        "stage_sems": DMA((4,)),
        "mixed_sems": DMA((4,)),
        "states_sems": DMA((4,)),
        "out_copy_sems": DMA((4,)),
        "load_sems": DMA((4,)),
        "stat_sems": DMA((2, 15)),
        "gate_sems": DMA((2, 15)),
        "dot_sems": DMA((2, 15)),
        "sum_sems": DMA((2, 7)),
        "normed_sems": DMA((2, 40)),
        "bgrad_sems": DMA((2, 40)),
        "out_sems": DMA((2, 40)),
        "norm_sems": DMA((2, 40)),
        "kv_sems": DMA((2, 8)),
        "kv_grad_sems": DMA((2, 8)),
        "wo_sems": DMA((2, 8)),
        "wq_sems": DMA((2, 8)),
        "wkv_sems": DMA((2, 8)),
    }
    table.update(scatter_scratch("kv", CAP, CAP))
    table.update(scatter_scratch("wo", 32, D))
    table.update(scatter_scratch("wq", CAP, 256))
    table.update(scatter_scratch("wkv", CAP, CAP))
    del table["wkv_part"]
    return table


INPUTS = (
    "picked", "gain", "router", "counts", "states", "upstream", "w_query", "w_key", "w_value", "w_output",
)
OUTPUTS = {
    "o_mixed": ((4, 2, 256, 256), BF16),
    "o_grad_states": ((4, 2, 256, 256), BF16),
    "o_grad_q": ((CAP, 256), F32),
    "o_grad_k": ((CAP, 256), F32),
    "o_grad_v": ((CAP, 256), F32),
    "o_grad_out": ((32, D), F32),
    "o_small": ((8, 256), F32),
}
COPIES = ("grad_out", "grad_q", "grad_k", "grad_v")


def layer_kernel(*refs):
    r = Refs()
    names = list(INPUTS) + list(OUTPUTS) + list(scratch_table())
    for name, ref in zip(names, refs, strict=True):
        setattr(r, name, ref)
    r.grad_q = r.acc.at[:, pl.ds(0, 256)]
    r.grad_kv = r.acc.at[:, pl.ds(256, CAP)]
    place = Place()
    r.stage_loads = [
        pltpu.make_async_copy(src, r.part.at[pl.ds(4 * i, 4)], r.stage_sems.at[i])
        for i, src in enumerate((r.states, r.upstream))
    ]
    r.base_loads = [
        pltpu.make_async_copy(src, r.bgrad.at[pl.ds(4 * i, 4)], r.stage_sems.at[2 + i])
        for i, src in enumerate((r.states, r.upstream))
    ]
    r.loads = [
        pltpu.make_async_copy(w, r.w_in.at[:, :, pl.ds(256 * i, 256)], r.load_sems.at[i])
        for i, w in enumerate((r.w_query, r.w_key, r.w_value))
    ]
    r.loads.append(pltpu.make_async_copy(r.w_output, r.w_out, r.load_sems.at[3]))
    out_copies = []

    def out_copy(name, src, dst):
        copy = pltpu.make_async_copy(src, dst, r.out_copy_sems.at[COPIES.index(name)])
        copy.start()
        out_copies.append(copy)

    r.out_copy = out_copy
    partners = [place.tp_peer(p) for p in range(1, 16)] + [place.ctx_peer(p) for p in range(1, 8)]
    greet(partners)
    for load in r.stage_loads + r.loads:
        load.start()
    forward_phase(place, r, partners)
    backward_phase(place, r)
    for copy in out_copies:
        copy.wait()
    for goal, hbm, sems in ((8, r.o_mixed, r.mixed_sems), (12, r.o_grad_states, r.states_sems)):
        for i in range(4):
            pltpu.make_async_copy(r.bgrad.at[goal + i], hbm.at[i], sems.at[i]).wait()


def layer(*arrays):
    vmem = pl.BlockSpec(memory_space=pltpu.VMEM)
    hbm = pl.BlockSpec(memory_space=pl.ANY)
    smem = pl.BlockSpec(memory_space=pltpu.SMEM)
    return pl.pallas_call(
        layer_kernel,
        out_shape=[jax.ShapeDtypeStruct(*spec) for spec in OUTPUTS.values()],
        in_specs=[vmem] * 3 + [smem] + [hbm] * 6,
        out_specs=[hbm] * 6 + [vmem],
        scratch_shapes=list(scratch_table().values()),
        compiler_params=pltpu.CompilerParams(
            collective_id=0, has_side_effects=True, vmem_limit_bytes=VMEM_LIMIT
        ),
        name="layer",
    )(*arrays)


VMEM_LIMIT = 63 << 20


def hand_out_kernel(*refs):
    srcs, small, dsts, gain, router = refs[:6], refs[6], refs[7:13], refs[13], refs[14]
    held, come, go = refs[15:21], refs[21], refs[22]
    loads = [pltpu.make_async_copy(s, h, come.at[i]) for i, (s, h) in enumerate(zip(srcs, held))]
    stores = [pltpu.make_async_copy(h, d, go.at[i]) for i, (h, d) in enumerate(zip(held, dsts))]
    for load in loads:
        load.start()
    gain[...] = small[0:1]
    router[...] = small[1:2]
    for load, store in zip(loads, stores):
        load.wait()
        store.start()
    for store in stores:
        store.wait()


def hand_out(*arrays):
    hbm = pl.BlockSpec(memory_space=pltpu.HBM)
    vmem = pl.BlockSpec(memory_space=pltpu.VMEM)
    line = jax.ShapeDtypeStruct((1, 256), F32)
    return pl.pallas_call(
        hand_out_kernel,
        out_shape=[jax.ShapeDtypeStruct(a.shape, a.dtype) for a in arrays[:6]] + [line, line],
        in_specs=[hbm] * 6 + [vmem],
        out_specs=[hbm] * 6 + [vmem] * 2,
        scratch_shapes=[vm(a.shape, a.dtype) for a in arrays[:6]] + [DMA((6,)), DMA((6,))],
        compiler_params=pltpu.CompilerParams(vmem_limit_bytes=60 << 20),
        name="hand_out",
    )(*arrays)


def body(
    states, picked, counts, norm_gain, router_weight, w_query, w_key, w_value, w_out, upstream
):
    mixed, grad_states, grad_q, grad_k, grad_v, grad_out, small = layer(
        picked,
        norm_gain,
        router_weight,
        counts,
        states.reshape(4, 2, 256, 256),
        upstream.reshape(4, 2, 256, 256),
        w_query.reshape(16, 256, 256),
        w_key.reshape(16, 256, 256),
        w_value.reshape(16, 256, 256),
        w_out,
    )
    *outs, grad_gain, grad_router = hand_out(
        mixed.reshape(states.shape),
        grad_states.reshape(states.shape),
        grad_q,
        grad_k,
        grad_v,
        grad_out,
        small,
    )
    return (*outs, grad_gain.reshape(256), grad_router.reshape(256))


def solution(mesh):
    placed = (
        P("ctx", "tp"),
        P("ctx"),
        P("ctx"),
        P("tp"),
        P("tp"),
        P(None, "tp"),
        P(None, "tp"),
        P(None, "tp"),
        P("tp", None),
        P("ctx", "tp"),
    )
    return jax.shard_map(
        body,
        mesh=mesh,
        in_specs=placed,
        out_specs=(
            P("ctx", "tp"),
            P("ctx", "tp"),
            P("ctx", "tp"),
            P("ctx", "tp"),
            P("ctx", "tp"),
            P(("tp", "ctx"), None),
            P("tp"),
            P("tp"),
        ),
        check_vma=False,
    )
```

time: 564 us -> 137 us (0.24); the launches traced: 558 us -> 137 us
  waiting for transfers between devices: 234 us -> 0 us
  Pallas kernels: 0 us -> 136 us
  matrix products: 120 us -> 0 us
  blocking collectives: 100 us -> 0 us
  other arithmetic: 67.3 us -> 0 us
  local copies, waits for them, and re-layouts: 19.6 us -> 0 us
  between operations: 15 us -> 1.29 us
    pallas_call x0 -> x2, Pallas kernels: none -> 136 us  [the longest x1 131 us: layer(): pl.pallas_call(layer_kernel, out_shape=[jax.ShapeDtypeStruct(*spec) for s...]
    dot_general x18 -> x0, matrix products: 109 us -> none  [the longest x1 20.8 us: body(): jnp.einsum('hqk,khd->qhd', score_grad, key_heads, preferred_element_type=...]
    all_gather x4 -> x0, waiting for transfers between devices: 99.1 us -> none  [the longest x1 58.1 us: body(): shard_piece = lax.all_gather(block_grad, 'tp', axis=1, tiled=True)]
    psum x1 -> x0, waiting for transfers between devices: 69.5 us -> none  [body(): lax.psum(norm_part.astype(jnp.bfloat16), 'tp').astype(jnp.float32)]
    reduce_scatter x4 -> x0, waiting for transfers between devices: 65.6 us -> none  [the longest x1 51.4 us: body(): lax.psum_scatter(partial_out.astype(jnp.bfloat16), 'tp', scatter_dimensio...]
    all_gather x3 -> x0, blocking collectives: 52.1 us -> none  [the longest x1 20.1 us: body(): lax.all_gather(norm_gain, 'tp', axis=0, tiled=True)]
    psum x2 -> x0, blocking collectives: 48.2 us -> none  [the longest x1 34.5 us: body(): gate_dot = lax.psum(gate_part, 'tp')]
    convert_element_type x11 -> x0, other arithmetic: 26.4 us -> none  [the longest x1 9.46 us: body(): (lifted / jnp.sum(lifted, axis=-1, keepdims=True)).astype(jnp.bfloat16)]
  transfers between devices with their start and end apart: 9 -> 0, of which waited for: 7 -> 0; matrix products, arithmetic and copies ran while one was open for 24% -> 0% of each run, Pallas kernels for 0% -> 0%
where the time goes in v1:
time: 137 us
  Pallas kernels  136 us (99%)
    pallas_call x1, Pallas kernels, layer(): pl.pallas_call(layer_kernel, out_shape=[jax.ShapeDtypeStruct(*spec) for s...  131 us
    pallas_call x1, Pallas kernels, hand_out(): pl.pallas_call(hand_out_kernel, out_shape=[jax.ShapeDtypeStruct(a.shape,...  4.59 us

profile of v1, /device:TPU:1, one launch (start us, length us, event | category | flops | bytes accessed | tf_op | source)
XLA Modules:
  0.0 137.1 jit_solution(15094391982443900496)
XLA Ops:
  1.3 131.2 %layer.1 = (bf16[4,2,256,256]{3,2,1,0:T(8,128)(2,1)}, bf16[4,2,256,256]{3,2,1,0:T(8,128)(2,1)}, f32[512,256]{1,0:T(8,128)}, f32[512,256]{1,0:T(8,128)}, f32[512,...) custom-call(s32[512]{0:T(512)} %refs_0_.1, bf16[256]{0:T(256)(128)(2,1)} %refs_1_.1, bf16[256]{0:T(256)(128)(2,1)} %refs_2_.1, ...), custom_call_target="tpu_custom_call" | custom-call | tf_op jit(solution)/shard_map/layer/pallas_call | solution.py:887
  132.5 4.6 %hand_out.1 = (bf16[2048,256]{1,0:T(8,128)(2,1)}, bf16[2048,256]{1,0:T(8,128)(2,1)}, f32[512,256]{1,0:T(8,128)}, f32[512,256]{1,0:T(8,128)}, f32[512,256]{1,0:T(...) custom-call(bf16[2048,256]{1,0:T(8,128)(2,1)} %bitcast.14, bf16[2048,256]{1,0:T(8,128)(2,1)} %bitcast.15, ...), custom_call_target="tpu_custom_call" | custom-call | tf_op jit(solution)/shard_map/hand_out/pallas_call | solution.py:923
